TPU v7x, 256 devices: a whole 4x4x8 slice. The times are simulated.
256 devices in a mesh: grp: 2 (over core), fsdp: 16 (over z_lo, x), seq: 8 (over z_hi, y).
Axes of the slice: x: 4, y: 4, z: 8 (z_hi: 2, z_lo: 4; z = z_hi * 4 + z_lo), core: 2. Of those that a mesh axis runs over, the one named last changes fastest.
Arguments:
- clip_input: bfloat16 [32, 1024, 3072], P(('grp', 'fsdp'), 'seq'), may hold values from -6 to 6
- qkv_input: bfloat16 [32, 1024, 6144], P(('grp', 'fsdp'), 'seq'), may hold values from -12 to 12
- prompt_states: bfloat16 [32, 512, 4096], P(('grp', 'fsdp'), 'seq'), may hold values from -6 to 6
- prompt_ids: int32 [32, 512], P(('grp', 'fsdp'), 'seq'), may hold values from 0 to 32127, as said below
- t5_gain: float32 [4096], replicated, may hold values from 0.1 to 1.9
- w_text: bfloat16 [4096, 4096], P('seq', ('grp', 'fsdp')), may hold values from -0.09375 to 0.09375
- w_out: bfloat16 [2048, 3072], P('seq', ('grp', 'fsdp')), may hold values from -0.125 to 0.125
- gate_table: bfloat16 [1000, 3072], replicated, may hold values from -6 to 6
- timesteps: int32 [32], P(('grp', 'fsdp')), may hold values from 0 to 999
- out_cotangent: bfloat16 [32, 1024, 3072], P(('grp', 'fsdp'), 'seq'), may hold values from -6 to 6
Outputs:
- block_out: bfloat16 [32, 1024, 3072], P(('grp', 'fsdp'), 'seq')
- qkv_grad: bfloat16 [32, 1024, 6144], P(('grp', 'fsdp'), 'seq')
- w_out_grad: float32 [2048, 3072], P('seq', ('grp', 'fsdp'))
Inputs may be any that keep to these rules, and one draw needn't show every extreme that they name: `prompt_ids`: each prompt is a run of ids from 1 to 32127 of 128 to 512 tokens followed by zeros; some prompt has no zeros.
All inputs are finite; a program needn't handle non-finite values.
Results may differ from a plain program's by a relative error of at most 0.03.
Values may be sent and summed in bfloat16 or wider, within the bound.
A program may use at most 128 MiB of HBM per device.

v0:
```python
import functools
import math

import jax
import jax.numpy as jnp
from jax import lax
from jax.experimental import pallas as pl
from jax.experimental.pallas import tpu as pltpu
from jax.sharding import PartitionSpec as P

H = 16
HD = 128
D = 3072
DT = 4096
LEN = 1024
PROMPT = 512
TOK = 128
PTOK = 64
HALF = 512
PHALF = 256
FEAT = 256
COLS = 96
KC = 512

MESH = pl.DeviceIdType.MESH
BF = jnp.bfloat16
F32 = jnp.float32

norm_eps = 1e-06
masked_score = -1e30
score_scale = 1.0 / math.sqrt(HD)
log2e = math.log2(math.e)

N_COPIES = 140


def nt(a, b):
    return lax.dot_general(a, b, (((1,), (1,)), ((), ())), preferred_element_type=F32)


def nn(a, b):
    return lax.dot_general(a, b, (((1,), (0,)), ((), ())), preferred_element_type=F32)


def body(
    gate, gain, cot, clip, prm, ids, wtin, woin, qkv,
    bo, dqo, wgo,
    wt, wo, pg, pgt, nrm, cnts, qkvs, dos, dosend, tkv, tksend,
    kb, vb, kt, vt, probs, att, aabs, dqs,
    pp, pa, pf, pown, wsend, wrecv, wxs, wxr, wzs, wzr,
    send_sem, recv_sem, loc_sem,
):
    g = lax.axis_index("grp")
    f = lax.axis_index("fsdp")
    s = lax.axis_index("seq")
    zlo, x = lax.div(f, 4), lax.rem(f, 4)
    zhi, y = lax.div(s, 4), lax.rem(s, 4)
    z = zhi * 4 + zlo
    ozhi = 1 - zhi

    def at(gg, xx, yy, zz):
        return (gg, lax.rem(zz, 4) * 4 + xx, lax.div(zz, 4) * 4 + yy)

    sib = at(1 - g, x, y, z)
    xd = [at(g, lax.rem(x + j, 4), y, z) for j in range(4)]
    yd = [at(g, x, lax.rem(y + j, 4), z) for j in range(4)]
    zd = [at(g, x, y, lax.rem(z + j, 8)) for j in range(8)]
    clip_peers = []
    for dz in range(2):
        for dy in range(4):
            if dz or dy:
                py, pz = lax.rem(y + dy, 4), lax.rem(z + 4 * dz, 8)
                clip_peers.append((at(g, x, py, pz), lax.div(pz, 4) * 4 + py))
    partner = zd[4]
    peers = [sib] + xd[1:] + zd[1:] + [clip_peers[i][0] for i in (0, 1, 2, 4, 5, 6)]

    barrier = pltpu.get_barrier_semaphore()
    for p in peers:
        pl.semaphore_signal(barrier, inc=1, device_id=p, device_id_type=MESH)

    started = []

    def send(src, dst, device):
        i = len(started)
        c = pltpu.make_async_remote_copy(
            src_ref=src, dst_ref=dst, send_sem=send_sem.at[i], recv_sem=recv_sem.at[i],
            device_id=device, device_id_type=MESH,
        )
        c.start()
        started.append(c)
        return c

    def slot(zz):
        d = lax.rem(zz - z + 8, 8)
        return jnp.minimum(2 * d, 15 - 2 * d)

    wo[g, x, 0] = woin[...]
    wt[g, x, 0] = wtin[...]
    gate_row = gate[...].astype(F32)
    my_rows = pl.ds(pl.multiple_of(y * TOK, TOK), TOK)
    pg[my_rows, :] = (gate_row * cot[...].astype(F32)).astype(BF)
    my_prompt = pl.ds(pl.multiple_of(y * PTOK, PTOK), PTOK)
    wide = prm[...].astype(F32)
    mean = jnp.mean(wide * wide, axis=-1, keepdims=True)
    nrm[my_prompt, :] = (wide * lax.rsqrt(mean + norm_eps) * gain[...]).astype(BF)
    live = jnp.sum((ids[...] != 0).astype(jnp.int32), axis=-1, keepdims=True)
    cnts[0] = jnp.broadcast_to(live, (8, 128))

    pl.semaphore_wait(barrier, len(peers))

    def zstep(buf, k):
        if k < 4:
            a, b = (0, 0) if k == 1 else (2 * k - 3, 2 * k - 2)
            return [
                send(buf.at[g, x, a], buf.at[g, x, 2 * k - 1], zd[1]),
                send(buf.at[g, x, b], buf.at[g, x, 2 * k], zd[7]),
            ]
        h = buf.shape[3] // 2
        top, bottom = pl.ds(0, h), pl.ds(h, h)
        return [
            send(buf.at[g, x, 5, top], buf.at[g, x, 7, top], zd[1]),
            send(buf.at[g, x, 6, bottom], buf.at[g, x, 7, bottom], zd[7]),
        ]

    groups = ((0, 1), (1, 2), (3, 2), (5, 2), (7, 1))

    def xfirst(buf, k):
        sl = pl.ds(*groups[k])
        mine = buf.at[g, x, sl]
        return [send(mine, mine, xd[1]), send(mine, mine, xd[3])]

    def xsecond(buf, k):
        first, n = groups[k]
        lx, rx = lax.rem(x + 3, 4), lax.rem(x + 1, 4)
        if n == 2:
            from_left, from_right = buf.at[g, lx, first], buf.at[g, rx, first + 1]
        else:
            h = buf.shape[3] // 2
            from_left = buf.at[g, lx, first, pl.ds(0, h)]
            from_right = buf.at[g, rx, first, pl.ds(h, h)]
        return [send(from_left, from_left, xd[1]), send(from_right, from_right, xd[3])]

    def to_sibling(buf, k):
        both = buf.at[g, :, pl.ds(*groups[k])]
        return [send(both, both, sib)]

    def got(copies):
        for c in copies:
            c.wait_recv()

    def yfirst(buf, n):
        mine = buf.at[pl.ds(pl.multiple_of(y * n, n), n), :]
        return [send(mine, mine, yd[1]), send(mine, mine, yd[3])]

    def ysecond(buf, n):
        h = n // 2
        from_left = buf.at[pl.ds(pl.multiple_of(lax.rem(y + 3, 4) * n, n), h), :]
        from_right = buf.at[pl.ds(pl.multiple_of(lax.rem(y + 1, 4) * n + h, h), h), :]
        return [send(from_left, from_left, yd[1]), send(from_right, from_right, yd[3])]

    zt, zo, xt, xt2, st = {}, {}, {}, {}, {}
    zt[1] = zstep(wt, 1)
    xt[0] = xfirst(wt, 0)
    zo[1] = zstep(wo, 1)
    pg1 = yfirst(pg, TOK)
    n1 = yfirst(nrm, PTOK)
    cnt_copies = [
        send(cnts.at[0], cnts.at[i + 1], dev) for i, (dev, _) in enumerate(clip_peers)
    ]
    my_token_rows = pl.ds(pl.multiple_of(s * TOK, TOK), TOK)
    own_qkv = pltpu.make_async_copy(
        qkv.at[:, pl.ds(pl.multiple_of(s * 768, 768), 768)], qkvs.at[my_token_rows, :], loc_sem.at[0]
    )
    own_qkv.start()

    for k in range(1, 5):
        got(zt[k])
        if k < 4:
            zt[k + 1] = zstep(wt, k + 1)
        xt[k] = xfirst(wt, k)
        got(zo[k])
        if k < 4:
            zo[k + 1] = zstep(wo, k + 1)
        if k == 3:
            qkv_copies = []
            for dev, ps in reversed(clip_peers):
                cols = pl.ds(pl.multiple_of(ps * 768, 768), 768)
                qkv_copies.append(send(qkv.at[:, cols], qkvs.at[my_token_rows, :], dev))
            got(pg1)
            pg2 = ysecond(pg, TOK)
        if k == 4:
            mine = wo.at[g, x]
            xo = [send(mine, mine, xd[1]), send(mine, mine, xd[3])]
            got(n1)
            n2 = ysecond(nrm, PTOK)
        got(xt[k - 1])
        xt2[k - 1] = xsecond(wt, k - 1)
        if k >= 2:
            got(xt2[k - 2])
            st[k - 2] = to_sibling(wt, k - 2)
    got(xt[4])
    xt2[4] = xsecond(wt, 4)
    for k in (3, 4):
        got(xt2[k])
        st[k] = to_sibling(wt, k)
    got(n2)
    got(xo)
    from_left = wo.at[g, lax.rem(x + 3, 4), pl.ds(0, 4)]
    from_right = wo.at[g, lax.rem(x + 1, 4), pl.ds(4, 4)]
    xo2 = [send(from_left, from_left, xd[1]), send(from_right, from_right, xd[3])]
    for k in range(5):
        got(st[k])

    def prompt_kv(zh, dst, row0):
        def rows(i, carry):
            acc = jnp.zeros((128, 512), F32)
            here = pl.ds(pl.multiple_of(i * 128, 128), 128)
            for gg in range(2):
                for q in range(4):
                    sl = slot(zh * 4 + q)
                    w = jnp.concatenate([wt[gg, xx, sl] for xx in range(4)], axis=1)
                    acc += nt(nrm[here, pl.ds((gg * 4 + q) * 512, 512)], w)
            dst[pl.ds(pl.multiple_of(row0 + i * 128, 128), 128), :] = acc.astype(BF)
            return carry

        lax.fori_loop(0, PHALF // 128, rows, 0)

    prompt_kv(ozhi, tksend, 0)
    tk_copy = send(tksend, tkv.at[pl.ds(pl.multiple_of(zhi * PHALF, PHALF), PHALF), :], partner)
    prompt_kv(zhi, tkv, zhi * PHALF)
    got(xo2)
    both = wo.at[g]
    so = send(both, both, sib)
    got(pg2)

    def turn(i, carry):
        c = pl.ds(pl.multiple_of(i * 128, 128), 128)
        pgt[c, :] = pg[:, c].T
        return carry

    lax.fori_loop(0, D // 128, turn, 0)
    so.wait_recv()

    def attended_grad(zh, dst, row0):
        def rows(i, carry):
            acc = jnp.zeros((TOK, FEAT), F32)
            here = pl.ds(pl.multiple_of(i * TOK, TOK), TOK)
            for gg in range(2):
                for q in range(4):
                    w = wo[gg, :, slot(zh * 4 + q)].reshape(4 * COLS, FEAT)
                    acc += nn(pg[here, pl.ds((gg * 4 + q) * 384, 384)], w)
            dst[pl.ds(pl.multiple_of(row0 + i * TOK, TOK), TOK), :] = acc.astype(BF)
            return carry

        lax.fori_loop(0, HALF // TOK, rows, 0)

    attended_grad(ozhi, dosend, 0)
    half_rows = pl.ds(pl.multiple_of(zhi * HALF, HALF), HALF)
    do_copy = send(dosend, dos.at[half_rows, :], partner)
    attended_grad(zhi, dos, zhi * HALF)

    got(cnt_copies)
    total = cnts[0]
    for i in range(1, 8):
        total += cnts[i]
    live_row = total[0:1, 0:1]
    own_qkv.wait()
    got(qkv_copies)
    tk_copy.wait_recv()

    for h in range(2):
        kb[h, pl.ds(0, LEN), :] = qkvs[:, pl.ds(h * 384 + 128, 128)]
        vb[h, pl.ds(0, LEN), :] = qkvs[:, pl.ds(h * 384 + 256, 128)]
        kb[h, pl.ds(LEN, PROMPT), :] = tkv[:, pl.ds(h * 256, 128)]
        vb[h, pl.ds(LEN, PROMPT), :] = tkv[:, pl.ds(h * 256 + 128, 128)]
        kt[h] = kb[h].T
        vt[h] = vb[h].T

    chunks = [(c, c + KC) for c in range(0, LEN + PROMPT, KC)]

    def forward(half):
        here = pl.ds(pl.multiple_of(half * HALF, HALF), HALF)
        for h in range(2):
            q = qkvs[here, pl.ds(h * 384, 128)]
            scores, peak = [], None
            for lo, hi in chunks:
                t = nt(kb[h, lo:hi, :], q) * (score_scale * log2e)
                if lo >= LEN:
                    row = lax.broadcasted_iota(jnp.int32, t.shape, 0) + (lo - LEN)
                    t = jnp.where(row < live_row, t, masked_score)
                top = jnp.max(t, axis=0, keepdims=True)
                peak = top if peak is None else jnp.maximum(peak, top)
                scores.append(t)
            weights, norm = [], None
            for t in scores:
                e = jnp.exp2(t - peak)
                part = jnp.sum(e, axis=0, keepdims=True)
                norm = part if norm is None else norm + part
                weights.append(e)
            inv = 1.0 / norm
            o_t = None
            for (lo, hi), e in zip(chunks, weights):
                p = (e * inv).astype(BF)
                probs[h, lo:hi, here] = p
                term = nn(vt[h, :, lo:hi], p)
                o_t = term if o_t is None else o_t + term
            att[here, pl.ds(h * 128, 128)] = o_t.T.astype(BF)

    def backward(h):
        q = qkvs[:, pl.ds(h * 384, 128)]
        do = dos[:, pl.ds(h * 128, 128)]
        prod = do.astype(F32) * att[:, pl.ds(h * 128, 128)].astype(F32)
        row_dot = jnp.sum(prod.T, axis=0, keepdims=True)
        dq_t = None
        for lo, hi in chunks:
            p = probs[h, lo:hi, :]
            ds = (p.astype(F32) * (nt(vb[h, lo:hi, :], do) - row_dot)).astype(BF)
            term = nn(kt[h, :, lo:hi], ds)
            dq_t = term if dq_t is None else dq_t + term
            if hi <= LEN:
                dqs[lo:hi, pl.ds(h * 384 + 128, 128)] = (nn(ds, q) * score_scale).astype(BF)
                dqs[lo:hi, pl.ds(h * 384 + 256, 128)] = nn(p, do).astype(BF)
        dqs[:, pl.ds(h * 384, 128)] = (dq_t * score_scale).T.astype(BF)

    forward(ozhi)
    theirs = pl.ds(pl.multiple_of(ozhi * HALF, HALF), HALF)
    att_copy = send(att.at[theirs, :], aabs.at[zhi], partner)
    forward(zhi)
    aabs[zhi] = att[half_rows, :]
    do_copy.wait_recv()
    dq_copies = []
    for h in range(2):
        backward(h)
        hq = pl.ds(h * 384, 384)
        out_cols = pl.ds(pl.multiple_of(s * 768 + h * 384, 384), 384)
        for dev, ps in reversed(clip_peers):
            rows = pl.ds(pl.multiple_of(ps * TOK, TOK), TOK)
            dq_copies.append(send(dqs.at[rows, hq], dqo.at[:, out_cols], dev))
        dqo[:, out_cols] = dqs[my_token_rows, hq]

    att_copy.wait_recv()

    def project(rows, put):
        for gg in range(2):
            for q in range(4):
                acc = None
                for zh in range(2):
                    w = wo[gg, :, slot(zh * 4 + q)].reshape(4 * COLS, FEAT)
                    term = nt(aabs[zh, rows, :], w)
                    acc = term if acc is None else acc + term
                put(pl.ds((gg * 4 + q) * 384, 384), acc)

    def project_for(j):
        def put(c, v):
            pp[j - 1, :, c] = v.astype(BF)

        project(pl.ds(pl.multiple_of(lax.rem(y + j, 4) * TOK, TOK), TOK), put)

    first, second = pl.ds(0, TOK // 2), pl.ds(TOK // 2, TOK // 2)
    project_for(2)
    p_far = [
        send(pp.at[1, first], pa.at[0], yd[1]),
        send(pp.at[1, second], pa.at[1], yd[3]),
    ]
    project_for(1)
    p_near = [send(pp.at[0, second], pf.at[0, second], yd[1])]
    project_for(3)
    p_near.append(send(pp.at[2, first], pf.at[1, first], yd[3]))

    def weight_grad(gg, put):
        def group(q, carry):
            rows = pl.ds(pl.multiple_of((gg * 4 + q) * 384, 384), 384)
            for zh in range(2):
                put(zh * 4 + q, nn(pgt[rows, :], aabs[zh]).reshape(4, COLS, FEAT))
            return carry

        lax.fori_loop(0, 4, group, 0)

    def put_sibling(zz, v):
        wsend[:, zz] = v.astype(BF)

    weight_grad(1 - g, put_sibling)
    w_copy = send(wsend, wrecv, sib)

    p_far[0].wait_recv()
    pp[0, first] = (pp[0, first].astype(F32) + pa[0].astype(F32)).astype(BF)
    p_near.append(send(pp.at[0, first], pf.at[0, first], yd[1]))
    p_far[1].wait_recv()
    pp[2, second] = (pp[2, second].astype(F32) + pa[1].astype(F32)).astype(BF)
    p_near.append(send(pp.at[2, second], pf.at[1, second], yd[3]))

    w_copy.wait_recv()

    def put_chip(zz, v):
        wxs[:, zz] = (v + wrecv[:, zz].astype(F32)).astype(BF)

    weight_grad(g, put_chip)
    wx_copies = [send(wxs.at[lax.rem(x + j, 4)], wxr.at[j - 1], xd[j]) for j in (2, 1, 3)]

    def put_own(c, v):
        pown[:, c] = v

    project(my_rows, put_own)

    got(wx_copies)

    def x_sum(i, carry):
        v = wxs[x, i].astype(F32)
        for j in range(3):
            v += wxr[j, i].astype(F32)
        wzs[i] = v.astype(BF)
        return carry

    lax.fori_loop(0, 8, x_sum, 0)
    wz_copies = [send(wzs.at[lax.rem(z + j, 8)], wzr.at[j - 1], zd[j]) for j in (4, 3, 5, 2, 6, 1, 7)]

    got(p_near)
    proj = pown[...] + pf[0].astype(F32) + pf[1].astype(F32)
    bo[...] = (clip[...].astype(F32) + gate_row * proj).astype(BF)

    got(wz_copies)
    v = wzs[z].astype(F32)
    for j in range(7):
        v += wzr[j].astype(F32)
    wgo[...] = v

    got(dq_copies)
    for c in started:
        c.wait_send()


def per_device(
    clip_input, qkv_input, prompt_states, prompt_ids, t5_gain, w_text, w_out, gate_table,
    timesteps, out_cotangent,
):
    gate_row = lax.dynamic_index_in_dim(gate_table, timesteps[0], 0, keepdims=True)
    vmem = pl.BlockSpec(memory_space=pltpu.VMEM)
    anym = pl.BlockSpec(memory_space=pl.ANY)
    vm = pltpu.VMEM
    scratch = [
        vm((2, 4, 8, 512, 128), BF),
        vm((2, 4, 8, COLS, FEAT), BF),
        vm((HALF, D), BF),
        vm((D, HALF), BF),
        vm((PHALF, DT), BF),
        vm((8, 8, 128), jnp.int32),
        vm((LEN, 768), BF),
        vm((LEN, FEAT), BF),
        vm((HALF, FEAT), BF),
        vm((PROMPT, 512), BF),
        vm((PHALF, 512), BF),
        vm((2, LEN + PROMPT, HD), BF),
        vm((2, LEN + PROMPT, HD), BF),
        vm((2, HD, LEN + PROMPT), BF),
        vm((2, HD, LEN + PROMPT), BF),
        vm((2, LEN + PROMPT, LEN), BF),
        vm((LEN, FEAT), BF),
        vm((2, HALF, FEAT), BF),
        vm((LEN, 768), BF),
        vm((3, TOK, D), BF),
        vm((2, TOK // 2, D), BF),
        vm((2, TOK, D), BF),
        vm((TOK, D), F32),
        vm((4, 8, COLS, FEAT), BF),
        vm((4, 8, COLS, FEAT), BF),
        vm((4, 8, COLS, FEAT), BF),
        vm((3, 8, COLS, FEAT), BF),
        vm((8, COLS, FEAT), BF),
        vm((7, COLS, FEAT), BF),
        pltpu.SemaphoreType.DMA((N_COPIES,)),
        pltpu.SemaphoreType.DMA((N_COPIES,)),
        pltpu.SemaphoreType.DMA((1,)),
    ]
    block_out, qkv_grad, w_grad_t = pl.pallas_call(
        body,
        out_shape=(
            jax.ShapeDtypeStruct((TOK, D), BF),
            jax.ShapeDtypeStruct((TOK, H * 3 * HD), BF),
            jax.ShapeDtypeStruct((COLS, FEAT), F32),
        ),
        in_specs=[vmem] * 8 + [anym],
        out_specs=(vmem, vmem, vmem),
        scratch_shapes=scratch,
        name="block",
        cost_estimate=pl.CostEstimate(flops=12_000_000_000, bytes_accessed=10_000_000, transcendentals=3_200_000),
        compiler_params=pltpu.CompilerParams(
            collective_id=0, has_side_effects=True, vmem_limit_bytes=60 * 1024 * 1024
        ),
    )(
        gate_row, t5_gain[None], out_cotangent[0], clip_input[0], prompt_states[0], prompt_ids,
        w_text, w_out.T, qkv_input[0],
    )
    return block_out[None], qkv_grad[None], w_grad_t.T


def solution(mesh):
    in_specs = (
        P(("grp", "fsdp"), "seq", None),
        P(("grp", "fsdp"), "seq", None),
        P(("grp", "fsdp"), "seq", None),
        P(("grp", "fsdp"), "seq"),
        P(),
        P("seq", ("grp", "fsdp")),
        P("seq", ("grp", "fsdp")),
        P(),
        P(("grp", "fsdp")),
        P(("grp", "fsdp"), "seq", None),
    )
    out_specs = (
        P(("grp", "fsdp"), "seq", None),
        P(("grp", "fsdp"), "seq", None),
        P("seq", ("grp", "fsdp")),
    )
    return jax.shard_map(
        per_device, mesh=mesh, in_specs=in_specs, out_specs=out_specs, check_vma=False
    )
```

profile of v0, /device:TPU:1, one launch (start us, length us, event | category | flops | bytes accessed | tf_op | source)
XLA Modules:
  0.0 168.9 jit_solution(11630589116880283996)
XLA Ops:
  1.3 1.4 constant_dynamic-slice_fusion.gate
  2.7 162.2 %block.1 = (bf16[128,3072]{1,0:T(8,128)(2,1)}, bf16[128,6144]{1,0:T(8,128)(2,1)}, f32[96,256]{1,0:T(8,128)}) custom-call(bf16[1,3072]{1,0:T(2,128)(2,1)} %constant_dynamic-slice_fusion.gate, f32[1,4096]{1,0:T(1,128)} %bitcast.21, bf16[128,3072]{1,0:T(8,128)(2,1)} %bitcast.17, bf16[128,3072]{1,0:T(8,128)(2,1)} %bitcast.18, bf16[64,4096]{1,0:T(8,128)(2,1)} %bitcast.19, ...), custom_call_target="tpu_custom_call" | custom-call | flops 12000000000 | bytes 10000000 | tf_op jit(solution)/shard_map/block/pallas_call | solution.py:474
  164.9 0.0 copy-start
  164.9 2.2 %copy.17 = bf16[1,128,3072]{2,1,0:T(8,128)(2,1)} copy(bf16[1,128,3072]{2,1,0:T(8,128)(2,1)} %bitcast.14) | data formatting | bytes 1572864
  167.1 0.0 copy-done
  167.1 0.0 copy-start.1
  167.1 1.1 copy.18
  168.3 0.0 copy-done.1
  168.3 0.6 copy.19
Async XLA Ops:
  164.9 2.2 %copy-start = (bf16[128,6144]{1,0:T(8,128)(2,1)S(1)}, bf16[128,6144]{1,0:T(8,128)(2,1)}, u32[]{:S(2)}) copy-start(bf16[128,6144]{1,0:T(8,128)(2,1)} %get-tuple-element.7) | copy-start | bytes 4718596
  167.1 1.1 copy-start.1
where the time goes:
time: 169 us
  Pallas kernels  162 us (96%)
  local copies, waits for them, and re-layouts  5.39 us (3%)
    pallas_call x1, Pallas kernels, per_device(): pl.pallas_call(body, out_shape=(jax.ShapeDtypeStruct((TOK, D), BF), jax.S...  162 us
    unnamed x7, local copies, waits for them, and re-layouts  3.97 us

commit v1 on v0

--- a/solution.py
+++ b/solution.py
@@ -96,16 +96,6 @@
 
     wo[g, x, 0] = woin[...]
     wt[g, x, 0] = wtin[...]
-    gate_row = gate[...].astype(F32)
-    my_rows = pl.ds(pl.multiple_of(y * TOK, TOK), TOK)
-    pg[my_rows, :] = (gate_row * cot[...].astype(F32)).astype(BF)
-    my_prompt = pl.ds(pl.multiple_of(y * PTOK, PTOK), PTOK)
-    wide = prm[...].astype(F32)
-    mean = jnp.mean(wide * wide, axis=-1, keepdims=True)
-    nrm[my_prompt, :] = (wide * lax.rsqrt(mean + norm_eps) * gain[...]).astype(BF)
-    live = jnp.sum((ids[...] != 0).astype(jnp.int32), axis=-1, keepdims=True)
-    cnts[0] = jnp.broadcast_to(live, (8, 128))
-
     pl.semaphore_wait(barrier, len(peers))
 
     def zstep(buf, k):
@@ -159,11 +149,33 @@
         return [send(from_left, from_left, yd[1]), send(from_right, from_right, yd[3])]
 
     zt, zo, xt, xt2, st = {}, {}, {}, {}, {}
+    qkv_copies = []
+
+    def send_qkv(peer, part=0, parts=1):
+        dev, ps = clip_peers[peer]
+        n = TOK // parts
+        qkv_copies.append(
+            send(
+                qkv.at[pl.ds(part * n, n), pl.ds(pl.multiple_of(ps * 768, 768), 768)],
+                qkvs.at[pl.ds(pl.multiple_of(s * TOK + part * n, n), n), :],
+                dev,
+            )
+        )
+
     zt[1] = zstep(wt, 1)
     xt[0] = xfirst(wt, 0)
     zo[1] = zstep(wo, 1)
-    pg1 = yfirst(pg, TOK)
+    send_qkv(3, 0, 4)
+    my_prompt = pl.ds(pl.multiple_of(y * PTOK, PTOK), PTOK)
+    wide = prm[...].astype(F32)
+    mean = jnp.mean(wide * wide, axis=-1, keepdims=True)
+    nrm[my_prompt, :] = (wide * lax.rsqrt(mean + norm_eps) * gain[...]).astype(BF)
     n1 = yfirst(nrm, PTOK)
+    gate_row = gate[...].astype(F32)
+    my_rows = pl.ds(pl.multiple_of(y * TOK, TOK), TOK)
+    pg[my_rows, :] = (gate_row * cot[...].astype(F32)).astype(BF)
+    live = jnp.sum((ids[...] != 0).astype(jnp.int32), axis=-1, keepdims=True)
+    cnts[0] = jnp.broadcast_to(live, (8, 128))
     cnt_copies = [
         send(cnts.at[0], cnts.at[i + 1], dev) for i, (dev, _) in enumerate(clip_peers)
     ]
@@ -181,83 +193,77 @@
         got(zo[k])
         if k < 4:
             zo[k + 1] = zstep(wo, k + 1)
-        if k == 3:
-            qkv_copies = []
-            for dev, ps in reversed(clip_peers):
-                cols = pl.ds(pl.multiple_of(ps * 768, 768), 768)
-                qkv_copies.append(send(qkv.at[:, cols], qkvs.at[my_token_rows, :], dev))
-            got(pg1)
-            pg2 = ysecond(pg, TOK)
-        if k == 4:
-            mine = wo.at[g, x]
-            xo = [send(mine, mine, xd[1]), send(mine, mine, xd[3])]
+            send_qkv(3, k, 4)
+        else:
+            for peer in (6, 5, 4):
+                send_qkv(peer)
+        if k == 2:
             got(n1)
             n2 = ysecond(nrm, PTOK)
+            pg1 = yfirst(pg, TOK)
         got(xt[k - 1])
         xt2[k - 1] = xsecond(wt, k - 1)
         if k >= 2:
             got(xt2[k - 2])
             st[k - 2] = to_sibling(wt, k - 2)
+    got(pg1)
+    pg2 = ysecond(pg, TOK)
+    for peer in (2, 1, 0):
+        send_qkv(peer)
     got(xt[4])
     xt2[4] = xsecond(wt, 4)
-    for k in (3, 4):
-        got(xt2[k])
-        st[k] = to_sibling(wt, k)
+    mine = wo.at[g, x]
+    xo = [send(mine, mine, xd[1]), send(mine, mine, xd[3])]
+    got(xt2[3])
+    st[3] = to_sibling(wt, 3)
+    got(xt2[4])
+    st[4] = to_sibling(wt, 4)
     got(n2)
+    for k in range(5):
+        got(st[k])
+
+    def prompt_kv(zh, dst, row0):
+        acc = jnp.zeros((PHALF, 512), F32)
+        for gg in range(2):
+            for q in range(4):
+                sl = slot(zh * 4 + q)
+                w = jnp.concatenate([wt[gg, xx, sl] for xx in range(4)], axis=1)
+                acc += nt(nrm[:, pl.ds((gg * 4 + q) * 512, 512)], w)
+        dst[pl.ds(pl.multiple_of(row0, PHALF), PHALF), :] = acc.astype(BF)
+
+    prompt_kv(ozhi, tksend, 0)
+    tk_copy = send(tksend, tkv.at[pl.ds(pl.multiple_of(zhi * PHALF, PHALF), PHALF), :], partner)
     got(xo)
     from_left = wo.at[g, lax.rem(x + 3, 4), pl.ds(0, 4)]
     from_right = wo.at[g, lax.rem(x + 1, 4), pl.ds(4, 4)]
     xo2 = [send(from_left, from_left, xd[1]), send(from_right, from_right, xd[3])]
-    for k in range(5):
-        got(st[k])
-
-    def prompt_kv(zh, dst, row0):
-        def rows(i, carry):
-            acc = jnp.zeros((128, 512), F32)
-            here = pl.ds(pl.multiple_of(i * 128, 128), 128)
-            for gg in range(2):
-                for q in range(4):
-                    sl = slot(zh * 4 + q)
-                    w = jnp.concatenate([wt[gg, xx, sl] for xx in range(4)], axis=1)
-                    acc += nt(nrm[here, pl.ds((gg * 4 + q) * 512, 512)], w)
-            dst[pl.ds(pl.multiple_of(row0 + i * 128, 128), 128), :] = acc.astype(BF)
-            return carry
-
-        lax.fori_loop(0, PHALF // 128, rows, 0)
-
-    prompt_kv(ozhi, tksend, 0)
-    tk_copy = send(tksend, tkv.at[pl.ds(pl.multiple_of(zhi * PHALF, PHALF), PHALF), :], partner)
     prompt_kv(zhi, tkv, zhi * PHALF)
     got(xo2)
     both = wo.at[g]
     so = send(both, both, sib)
     got(pg2)
 
+    so.wait_recv()
+
+    def attended_grad(zh, dst, row0):
+        acc = jnp.zeros((HALF, FEAT), F32)
+        for gg in range(2):
+            for q in range(4):
+                w = wo[gg, :, slot(zh * 4 + q)].reshape(4 * COLS, FEAT)
+                acc += nn(pg[:, pl.ds((gg * 4 + q) * 384, 384)], w)
+        dst[pl.ds(pl.multiple_of(row0, HALF), HALF), :] = acc.astype(BF)
+
+    attended_grad(ozhi, dosend, 0)
+    half_rows = pl.ds(pl.multiple_of(zhi * HALF, HALF), HALF)
+    do_copy = send(dosend, dos.at[half_rows, :], partner)
+    attended_grad(zhi, dos, zhi * HALF)
+
     def turn(i, carry):
         c = pl.ds(pl.multiple_of(i * 128, 128), 128)
         pgt[c, :] = pg[:, c].T
         return carry
 
     lax.fori_loop(0, D // 128, turn, 0)
-    so.wait_recv()
-
-    def attended_grad(zh, dst, row0):
-        def rows(i, carry):
-            acc = jnp.zeros((TOK, FEAT), F32)
-            here = pl.ds(pl.multiple_of(i * TOK, TOK), TOK)
-            for gg in range(2):
-                for q in range(4):
-                    w = wo[gg, :, slot(zh * 4 + q)].reshape(4 * COLS, FEAT)
-                    acc += nn(pg[here, pl.ds((gg * 4 + q) * 384, 384)], w)
-            dst[pl.ds(pl.multiple_of(row0 + i * TOK, TOK), TOK), :] = acc.astype(BF)
-            return carry
-
-        lax.fori_loop(0, HALF // TOK, rows, 0)
-
-    attended_grad(ozhi, dosend, 0)
-    half_rows = pl.ds(pl.multiple_of(zhi * HALF, HALF), HALF)
-    do_copy = send(dosend, dos.at[half_rows, :], partner)
-    attended_grad(zhi, dos, zhi * HALF)
 
     got(cnt_copies)
     total = cnts[0]
@@ -329,16 +335,24 @@
     aabs[zhi] = att[half_rows, :]
     do_copy.wait_recv()
     dq_copies = []
+
+    def send_grad(h, dev, ps):
+        rows = pl.ds(pl.multiple_of(ps * TOK, TOK), TOK)
+        cols = pl.ds(pl.multiple_of(s * 768 + h * 384, 384), 384)
+        dq_copies.append(send(dqs.at[rows, pl.ds(h * 384, 384)], dqo.at[:, cols], dev))
+
     for h in range(2):
         backward(h)
-        hq = pl.ds(h * 384, 384)
-        out_cols = pl.ds(pl.multiple_of(s * 768 + h * 384, 384), 384)
-        for dev, ps in reversed(clip_peers):
-            rows = pl.ds(pl.multiple_of(ps * TOK, TOK), TOK)
-            dq_copies.append(send(dqs.at[rows, hq], dqo.at[:, out_cols], dev))
-        dqo[:, out_cols] = dqs[my_token_rows, hq]
+        for dev, ps in clip_peers[:3]:
+            send_grad(h, dev, ps)
+        dqo[:, pl.ds(pl.multiple_of(s * 768 + h * 384, 384), 384)] = dqs[
+            my_token_rows, pl.ds(h * 384, 384)
+        ]
 
     att_copy.wait_recv()
+    for h in range(2):
+        for dev, ps in reversed(clip_peers[3:]):
+            send_grad(h, dev, ps)
 
     def project(rows, put):
         for gg in range(2):
@@ -357,6 +371,20 @@
         project(pl.ds(pl.multiple_of(lax.rem(y + j, 4) * TOK, TOK), TOK), put)
 
     first, second = pl.ds(0, TOK // 2), pl.ds(TOK // 2, TOK // 2)
+    def weight_grad(gg, put):
+        def group(q, carry):
+            rows = pl.ds(pl.multiple_of((gg * 4 + q) * 384, 384), 384)
+            for zh in range(2):
+                put(zh * 4 + q, nn(pgt[rows, :], aabs[zh]).reshape(4, COLS, FEAT))
+            return carry
+
+        lax.fori_loop(0, 4, group, 0)
+
+    def put_sibling(zz, v):
+        wsend[:, zz] = v.astype(BF)
+
+    weight_grad(1 - g, put_sibling)
+    w_copy = send(wsend, wrecv, sib)
     project_for(2)
     p_far = [
         send(pp.at[1, first], pa.at[0], yd[1]),
@@ -367,20 +395,13 @@
     project_for(3)
     p_near.append(send(pp.at[2, first], pf.at[1, first], yd[3]))
 
-    def weight_grad(gg, put):
-        def group(q, carry):
-            rows = pl.ds(pl.multiple_of((gg * 4 + q) * 384, 384), 384)
-            for zh in range(2):
-                put(zh * 4 + q, nn(pgt[rows, :], aabs[zh]).reshape(4, COLS, FEAT))
-            return carry
-
-        lax.fori_loop(0, 4, group, 0)
-
-    def put_sibling(zz, v):
-        wsend[:, zz] = v.astype(BF)
-
-    weight_grad(1 - g, put_sibling)
-    w_copy = send(wsend, wrecv, sib)
+    w_copy.wait_recv()
+
+    def put_chip(zz, v):
+        wxs[:, zz] = (v + wrecv[:, zz].astype(F32)).astype(BF)
+
+    weight_grad(g, put_chip)
+    wx_copies = [send(wxs.at[lax.rem(x + j, 4)], wxr.at[j - 1], xd[j]) for j in (2, 1, 3)]
 
     p_far[0].wait_recv()
     pp[0, first] = (pp[0, first].astype(F32) + pa[0].astype(F32)).astype(BF)
@@ -388,14 +409,6 @@
     p_far[1].wait_recv()
     pp[2, second] = (pp[2, second].astype(F32) + pa[1].astype(F32)).astype(BF)
     p_near.append(send(pp.at[2, second], pf.at[1, second], yd[3]))
-
-    w_copy.wait_recv()
-
-    def put_chip(zz, v):
-        wxs[:, zz] = (v + wrecv[:, zz].astype(F32)).astype(BF)
-
-    weight_grad(g, put_chip)
-    wx_copies = [send(wxs.at[lax.rem(x + j, 4)], wxr.at[j - 1], xd[j]) for j in (2, 1, 3)]
 
     def put_own(c, v):
         pown[:, c] = v

time: 169 us -> 164 us (0.970)
  Pallas kernels: 162 us -> 156 us
    pallas_call x1, Pallas kernels: 162 us -> 156 us  [per_device(): pl.pallas_call(body, out_shape=(jax.ShapeDtypeStruct((TOK, D), BF), jax.S...]
where the time goes in v1:
time: 164 us; the launch traced here: 163 us
  Pallas kernels  156 us (95%)
  local copies, waits for them, and re-layouts  5.39 us (3%)
    pallas_call x1, Pallas kernels, per_device(): pl.pallas_call(body, out_shape=(jax.ShapeDtypeStruct((TOK, D), BF), jax.S...  156 us
    unnamed x7, local copies, waits for them, and re-layouts  3.97 us

profile of v1, /device:TPU:1, one launch (start us, length us, event | category | flops | bytes accessed | tf_op | source)
XLA Modules:
  0.0 162.6 jit_solution(4231671930992461956)
XLA Ops:
  1.3 1.4 constant_dynamic-slice_fusion.gate
  2.7 156.0 %block.1 = (bf16[128,3072]{1,0:T(8,128)(2,1)}, bf16[128,6144]{1,0:T(8,128)(2,1)}, f32[96,256]{1,0:T(8,128)}) custom-call(bf16[1,3072]{1,0:T(2,128)(2,1)} %constant_dynamic-slice_fusion.gate, f32[1,4096]{1,0:T(1,128)} %bitcast.21, bf16[128,3072]{1,0:T(8,128)(2,1)} %bitcast.17, bf16[128,3072]{1,0:T(8,128)(2,1)} %bitcast.18, bf16[64,4096]{1,0:T(8,128)(2,1)} %bitcast.19, ...), custom_call_target="tpu_custom_call" | custom-call | flops 12000000000 | bytes 10000000 | tf_op jit(solution)/shard_map/block/pallas_call | solution.py:487
  158.7 0.0 copy-start
  158.7 2.2 %copy.17 = bf16[1,128,3072]{2,1,0:T(8,128)(2,1)} copy(bf16[1,128,3072]{2,1,0:T(8,128)(2,1)} %bitcast.14) | data formatting | bytes 1572864
  160.9 0.0 copy-done
  160.9 0.0 copy-start.1
  160.9 1.1 copy.18
  162.0 0.0 copy-done.1
  162.0 0.6 copy.19
Async XLA Ops:
  158.7 2.2 %copy-start = (bf16[128,6144]{1,0:T(8,128)(2,1)S(1)}, bf16[128,6144]{1,0:T(8,128)(2,1)}, u32[]{:S(2)}) copy-start(bf16[128,6144]{1,0:T(8,128)(2,1)} %get-tuple-element.7) | copy-start | bytes 4718596
  160.9 1.1 copy-start.1
